TPU v7x, 32 devices: a whole 2x2x4 slice. The times are simulated.
32 devices in a mesh: groups: 2 (over x), ctx: 16 (over z, y, core).
Axes of the slice: x: 2, y: 2, z: 4, core: 2. Of those that a mesh axis runs over, the one named last changes fastest.
Arguments:
- hidden: bfloat16 [24576, 4096], P(('groups', 'ctx')), parts along dimension 0, may hold values from -6 to 6
- w_qkv: bfloat16 [4096, 768], P('ctx'), may hold values from -0.09375 to 0.09375
- w_out: bfloat16 [256, 4096], P('ctx'), may hold values from -0.375 to 0.375
- norm_gain: float32 [256], replicated, may hold values from 0.1 to 1.9
- incoming: float32 [4, 128, 128], P('groups'), parts along dimension 0, may hold values from -600 to 600
Outputs:
- attn_out: bfloat16 [24576, 4096], P(('groups', 'ctx')), parts along dimension 0
There are 2 independent parts, one for each index of `groups`. A program takes and returns all parts, laid end to end along the dimension named above; an argument that names none is the same for every part. Nothing has to cross between parts.
All inputs are finite; a program needn't handle non-finite values.
Results may differ from a plain program's by a relative error of at most 0.0065.
Values may be sent and summed in bfloat16 or wider, within the bound.
A program may use at most 64 MiB of HBM per device.

v0:
```python
import jax
import jax.numpy as jnp
from jax import lax
from jax.sharding import PartitionSpec as P


def carried_in(value, axis, join, neutral):
    count, mine = (lax.axis_size(axis), lax.axis_index(axis))
    pieces = lax.all_gather(value, axis)
    running = jnp.full_like(value, 0) + jnp.asarray(neutral, value.dtype)

    def turn(position, running):
        longer = join(running, pieces[position])
        return jnp.where(position < mine, longer, running)

    return lax.fori_loop(0, count - 1, turn, running)


def local(hidden, w_qkv, w_out, norm_gain, incoming):
    tokens_here = hidden.shape[0]
    width = w_qkv.shape[1] // 3
    heads = incoming.shape[0]
    head_size = incoming.shape[1]
    columns = hidden
    proj = jnp.dot(
        columns,
        lax.all_gather(w_qkv, "ctx", axis=0, tiled=True),
        preferred_element_type=jnp.float32,
    ).astype(jnp.bfloat16)
    query = proj[:, :width].reshape(tokens_here, heads, head_size)
    keys = proj[:, width : 2 * width].reshape(tokens_here, heads, head_size)
    values = proj[:, 2 * width :].reshape(tokens_here, heads, head_size)
    state = jnp.einsum("thd,the->hde", keys, values, preferred_element_type=jnp.float32)
    zero_state = jnp.zeros_like(state)

    def add_states(earlier, later):
        return earlier + later

    before = carried_in(state, "ctx", add_states, zero_state)
    prior = incoming + before
    scores = jnp.einsum("thd,shd->hts", query, keys, preferred_element_type=jnp.float32)
    rows = jnp.arange(tokens_here)
    causal = rows[:, None] >= rows[None, :]
    scores = jnp.where(causal[None], scores, 0.0).astype(jnp.bfloat16)
    intra = jnp.einsum("hts,she->the", scores, values, preferred_element_type=jnp.float32)
    cross = jnp.einsum(
        "thd,hde->the", query.astype(jnp.float32), prior, precision=lax.Precision.HIGHEST
    )
    mixed = intra + cross
    scale = lax.rsqrt(jnp.mean(mixed * mixed, axis=-1, keepdims=True) + 1e-06)
    gains = norm_gain.reshape(heads, head_size)
    normed = (mixed * scale * gains).astype(jnp.bfloat16).reshape(tokens_here, width)
    columns = normed
    result = jnp.dot(
        columns,
        lax.all_gather(w_out, "ctx", axis=0, tiled=True),
        preferred_element_type=jnp.float32,
    )
    return result.astype(jnp.bfloat16)


def solution(mesh):
    return jax.shard_map(
        local,
        mesh=mesh,
        in_specs=(
            P(("groups", "ctx"), None),
            P("ctx", None),
            P("ctx", None),
            P(),
            P("groups", None, None),
        ),
        out_specs=P(("groups", "ctx"), None),
        check_vma=False,
    )
```

profile of v0, /device:TPU:0, one launch (start us, length us, event | category | flops | bytes accessed | tf_op | source)
XLA Modules:
  0.0 179.5 jit_solution(12376154910145856354)
XLA Ops:
  6.5 0.7 all-gather.5.cloned.1.call-update
  7.3 0.0 all-gather.9.cloned.1.call-start
  7.3 66.9 %all-gather.5.cloned.1.call-done = bf16[4096,768]{1,0:T(8,128)(2,1)} async-done(((bf16[256,768]{1,0:T(8,128)(2,1)}), bf16[4096,768]{1,0:T(8,128)(2,1)}) %all-gather.5.cloned.1.call-update) | async-done | bytes 6291472 | tf_op jit(solution)/shard_map/all_gather | solution.py:27
  74.2 9.1 %convolution_convert_fusion.1 = bf16[768,768]{0,1:T(8,128)(2,1)S(1)} fusion(bf16[768,4096]{1,0:T(8,128)(2,1)} %param.7, bf16[4096,768]{1,0:T(8,128)(2,1)} %all-gather.5.cloned.1.call-done), kind=kOutput, calls=%fused_computation.8 | convolution fusion | flops 4832428032 | bytes 13762560 | tf_op jit(solution)/shard_map/dot_general | solution.py:25
  83.3 0.1 fusion.10
  83.4 0.9 fusion.11
  84.3 0.0 all-gather.9.cloned.1.call-update
  84.3 0.0 all-gather.7.cloned.1.call-start
  84.4 0.7 all-gather.7.cloned.1.call-update
  85.1 0.2 iota_compare_fusion
  85.3 39.2 %all-gather.9.cloned.1.call-done = f32[32,128,128]{2,1,0:T(8,128)} async-done(((f32[2,128,128]{2,1,0:T(8,128)}), f32[32,128,128]{2,1,0:T(8,128)}) %all-gather.9.cloned.1.call-update) | async-done | bytes 2097168 | tf_op jit(solution)/shard_map/all_gather | solution.py:9
  124.5 14.6 %while.14 = (s32[]{:T(128)}, f32[2,128,128]{2,1,0:T(8,128)S(1)}, s32[]{:T(128)}, f32[16,2,128,128]{3,2,1,0:T(8,128)}, s32[]{:T(128)}, /*index=5*/s32[]{:T(128)}) while((s32[]{:T(128)}, f32[2,128,128]{2,1,0:T(8,128)S(1)}, s32[]{:T(128)}, f32[16,2,128,128]{3,2,1,0:T(8,128)}, s32[]{:T(128)}, /*index=5*/s32[]{:T(128)}) %tuple.44), condition=%wide.region_1.2_spmd.clone, body=%wide.region_0.1_spmd.clone.sunk | while | flops 98308 | bytes 393317 | solution.py:16
  124.5 0.9 add_select_fusion.2
  125.5 0.9 add_select_fusion.2
  126.4 0.9 add_select_fusion.2
  127.4 0.9 add_select_fusion.2
  128.4 0.9 add_select_fusion.2
  129.4 0.9 add_select_fusion.2
  130.3 0.9 add_select_fusion.2
  131.3 0.9 add_select_fusion.2
  132.3 1.0 add_select_fusion.2
  133.3 1.0 add_select_fusion.2
  134.2 0.9 add_select_fusion.2
  135.2 0.9 add_select_fusion.2
  136.2 0.9 add_select_fusion.2
  137.2 0.9 add_select_fusion.2
  138.1 1.0 add_select_fusion.2
  139.1 0.5 fusion.7
  139.7 1.6 multiply_reduce_fusion
  141.3 0.1 multiply_convert_fusion
  141.4 25.4 %all-gather.7.cloned.1.call-done = bf16[256,4096]{1,0:T(8,128)(2,1)} async-done(((bf16[16,4096]{1,0:T(8,128)(2,1)}), bf16[256,4096]{1,0:T(8,128)(2,1)}) %all-gather.7.cloned.1.call-update) | async-done | bytes 2097168 | tf_op jit(solution)/shard_map/all_gather | solution.py:56
  166.8 6.1 %convolution_convert_fusion = bf16[768,4096]{1,0:T(8,128)(2,1)} fusion(bf16[768,256]{0,1:T(8,128)(2,1)S(1)} %bitcast.22, bf16[256,4096]{1,0:T(8,128)(2,1)} %all-gather.7.cloned.1.call-done), kind=kOutput, calls=%fused_computation.1 | convolution fusion | flops 1613758464 | bytes 8781824 | tf_op jit(solution)/shard_map/dot_general | solution.py:54
  (7 shorter events, 0.0 us)
Async XLA Ops:
  6.5 67.7 %all-gather.5.cloned.1.call-start = ((), (), s32[]{:S(2)}) async-start(), calls=%async_computation | async-start | bytes 6684672 | tf_op jit(solution)/shard_map/all_gather | solution.py:27
  7.3 117.2 %all-gather.9.cloned.1.call-start = ((), (), s32[]{:S(2)}) async-start(), calls=%async_computation.2 | async-start | bytes 2228224 | tf_op jit(solution)/shard_map/all_gather | solution.py:9
  83.4 55.7 %copy-start = (f32[2,128,128]{2,1,0:T(8,128)S(1)}, f32[2,128,128]{2,1,0:T(8,128)}, u32[]{:S(2)}) copy-start(f32[2,128,128]{2,1,0:T(8,128)} %param.11) | copy-start | bytes 393220
  84.3 82.5 %all-gather.7.cloned.1.call-start = ((), (), s32[]{:S(2)}) async-start(), calls=%async_computation.1 | async-start | bytes 2228224 | tf_op jit(solution)/shard_map/all_gather | solution.py:56
  139.6 1.7 copy-start.1
Sparse Core Ops, SparseCore 0:
  9.6 64.5 all-gather.4
  84.5 39.9 all-gather.8
  126.7 40.0 all-gather.6
where the time goes:
time: 180 us; the launch traced here: 179 us
  waiting for transfers between devices  133 us (74%)
  matrix products  18.3 us (10%)
  other arithmetic  14.6 us (8%)
  between operations  13.2 us (7%)
    all_gather x1, waiting for transfers between devices, local(): lax.all_gather(w_qkv, 'ctx', axis=0, tiled=True)  66.9 us
    all_gather x1, waiting for transfers between devices, carried_in(): pieces = lax.all_gather(value, axis)  39.2 us
    all_gather x1, waiting for transfers between devices, local(): lax.all_gather(w_out, 'ctx', axis=0, tiled=True)  25.4 us
    select_n x15, other arithmetic, turn(): return jnp.where(position < mine, longer, running)  14.3 us
    dot_general x1, matrix products, local(): jnp.dot(columns, lax.all_gather(w_qkv, 'ctx', axis=0, tiled=True), prefer...  9.06 us
    dot_general x1, matrix products, local(): jnp.dot(columns, lax.all_gather(w_out, 'ctx', axis=0, tiled=True), prefer...  6.12 us
  transfers between devices with their start and end apart: 3, of which 3 were waited for; matrix products, arithmetic and copies ran while one was open for 9% of the time, Pallas kernels for 0%

commit v1 on v0

--- a/solution.py
+++ b/solution.py
@@ -2,6 +2,24 @@
 import jax.numpy as jnp
 from jax import lax
 from jax.sharding import PartitionSpec as P
+
+
+def gather_around(value, axis, dim):
+    ways, here, step = (lax.axis_size(axis), lax.axis_index(axis), value.shape[dim])
+    dims = [n * ways if d == dim else n for d, n in enumerate(value.shape)]
+    full = lax.dynamic_update_slice_in_dim(
+        jnp.zeros(dims, value.dtype), value, here * step, axis=dim
+    )
+    going_up = going_down = value
+    for far in range(1, ways // 2 + 1):
+        going_up = lax.ppermute(going_up, axis, [(d, (d + 1) % ways) for d in range(ways)])
+        full = lax.dynamic_update_slice_in_dim(full, going_up, (here - far) % ways * step, axis=dim)
+        if 2 * far < ways:
+            going_down = lax.ppermute(going_down, axis, [(d, (d - 1) % ways) for d in range(ways)])
+            full = lax.dynamic_update_slice_in_dim(
+                full, going_down, (here + far) % ways * step, axis=dim
+            )
+    return full
 
 
 def carried_in(value, axis, join, neutral):
@@ -51,11 +69,7 @@
     gains = norm_gain.reshape(heads, head_size)
     normed = (mixed * scale * gains).astype(jnp.bfloat16).reshape(tokens_here, width)
     columns = normed
-    result = jnp.dot(
-        columns,
-        lax.all_gather(w_out, "ctx", axis=0, tiled=True),
-        preferred_element_type=jnp.float32,
-    )
+    result = jnp.dot(columns, gather_around(w_out, "ctx", 0), preferred_element_type=jnp.float32)
     return result.astype(jnp.bfloat16)
 
 

time: 180 us -> 163 us (0.906)
  waiting for transfers between devices: 133 us -> 77.4 us
  starting transfers between devices: 0.08 us -> 30.2 us
  local copies, waits for them, and re-layouts: 0.09 us -> 3.26 us
  matrix products: 18.3 us -> 20.6 us
  other arithmetic: 14.6 us -> 16.5 us
    all_gather x1, waiting for transfers between devices: 66.9 us -> 29.5 us  [local(): lax.all_gather(w_qkv, 'ctx', axis=0, tiled=True)]
    ppermute x0 -> x15, waiting for transfers between devices: none -> 30.8 us  [the longest x8 16 us: gather_around(): lax.ppermute(going_up, axis, [(d, (d + 1) % ways) for d in range(ways)])]
    ppermute x0 -> x15, starting transfers between devices: none -> 30.1 us  [the longest x7 30.1 us: gather_around(): lax.ppermute(going_down, axis, [(d, (d - 1) % ways) for d in range(ways)])]
    all_gather x1 -> x0, waiting for transfers between devices: 25.4 us -> none  [local(): lax.all_gather(w_out, 'ctx', axis=0, tiled=True)]
    all_gather x1, waiting for transfers between devices: 39.2 us -> 16.4 us  [carried_in(): pieces = lax.all_gather(value, axis)]
    dynamic_update_slice x0 -> x16, local copies, waits for them, and re-layouts: none -> 2.95 us  [the longest x8 1.91 us: gather_around(): lax.dynamic_update_slice_in_dim(full, going_up, (here - far) % ways * ste...]
    dot_general x1, matrix products: 1.63 us -> 3.81 us  [local(): jnp.einsum('hts,she->the', scores, values, preferred_element_type=jnp.flo...]
  transfers between devices with their start and end apart: 3 -> 17, of which waited for: 3 -> 12; matrix products, arithmetic and copies ran while one was open for 9% -> 9% of each run, Pallas kernels for 0% -> 0%
where the time goes in v1:
time: 163 us; the launch traced here: 162 us
  waiting for transfers between devices  77.4 us (47%)
  starting transfers between devices  30.2 us (19%)
  matrix products  20.6 us (13%)
  other arithmetic  16.5 us (10%)
  between operations  13.8 us (8%)
  local copies, waits for them, and re-layouts  3.26 us (2%)
    ppermute x7, starting transfers between devices, gather_around(): lax.ppermute(going_down, axis, [(d, (d - 1) % ways) for d in range(ways)])  30.1 us
    all_gather x1, waiting for transfers between devices, local(): lax.all_gather(w_qkv, 'ctx', axis=0, tiled=True)  29.5 us
    all_gather x1, waiting for transfers between devices, carried_in(): pieces = lax.all_gather(value, axis)  16.4 us
    ppermute x8, waiting for transfers between devices, gather_around(): lax.ppermute(going_up, axis, [(d, (d + 1) % ways) for d in range(ways)])  16 us
    ppermute x7, waiting for transfers between devices, gather_around(): lax.ppermute(going_down, axis, [(d, (d - 1) % ways) for d in range(ways)])  14.8 us
    select_n x15, other arithmetic, turn(): return jnp.where(position < mine, longer, running)  14.2 us
    dot_general x1, matrix products, local(): jnp.dot(columns, lax.all_gather(w_qkv, 'ctx', axis=0, tiled=True), prefer...  9.06 us
    dot_general x1, matrix products, local(): jnp.dot(columns, gather_around(w_out, 'ctx', 0), preferred_element_type=j...  4.55 us
  transfers between devices with their start and end apart: 17, of which 12 were waited for; matrix products, arithmetic and copies ran while one was open for 9% of the time, Pallas kernels for 0%

profile of v1, /device:TPU:0, one launch (start us, length us, event | category | flops | bytes accessed | tf_op | source)
XLA Modules:
  0.0 162.1 jit_solution(17767712583549779066)
XLA Ops:
  7.3 5.5 %collective-permute-start.1 = (bf16[16,4096]{1,0:T(8,128)(2,1)}, bf16[16,4096]{1,0:T(8,128)(2,1)S(1)}, u32[]{:S(2)}, u32[]{:S(2)}) collective-permute-start(bf16[16,4096]{1,0:T(8,128)(2,1)} %param.9), channel_id=1, source_target_pairs={{0,15},{1,0},{2,1},{3,2},{4,3},{5,4},{6,5},{7,6},{8,7},{9,8},{10,9... | collective-permute-start | bytes 393224 | tf_op jit(solution)/shard_map/ppermute | solution.py:18
  13.3 1.0 iota_compare_fusion
  14.3 1.4 collective-permute-done.1
  15.6 4.5 %collective-permute-start.3 = (bf16[16,4096]{1,0:T(8,128)(2,1)S(1)}, bf16[16,4096]{1,0:T(8,128)(2,1)S(1)}, u32[]{:S(2)}, u32[]{:S(2)}) collective-permute-start(bf16[16,4096]{1,0:T(8,128)(2,1)S(1)} %collective-permute-done.1), channel_id=1, source_target_pairs={{0,15},{1,0},{2,1},{3,2},{4,3},{5,4},{6,5},{7,6},{8,7},{9,8},{10,9... | collective-permute-start | bytes 393224 | tf_op jit(solution)/shard_map/ppermute | solution.py:18
  20.1 5.2 %collective-permute-done.3 = bf16[16,4096]{1,0:T(8,128)(2,1)S(1)} collective-permute-done((bf16[16,4096]{1,0:T(8,128)(2,1)S(1)}, bf16[16,4096]{1,0:T(8,128)(2,1)S(1)}, u32[]{:S(2)}, u32[]{:S(2)}) %collective-permute-start.3) | collective-permute-done | bytes 131104 | tf_op jit(solution)/shard_map/ppermute | solution.py:18
  25.3 4.6 %collective-permute-start.5 = (bf16[16,4096]{1,0:T(8,128)(2,1)S(1)}, bf16[16,4096]{1,0:T(8,128)(2,1)S(1)}, u32[]{:S(2)}, u32[]{:S(2)}) collective-permute-start(bf16[16,4096]{1,0:T(8,128)(2,1)S(1)} %collective-permute-done.3), channel_id=1, source_target_pairs={{0,15},{1,0},{2,1},{3,2},{4,3},{5,4},{6,5},{7,6},{8,7},{9,8},{10,9... | collective-permute-start | bytes 393224 | tf_op jit(solution)/shard_map/ppermute | solution.py:18
  30.0 5.0 %collective-permute-done.5 = bf16[16,4096]{1,0:T(8,128)(2,1)S(1)} collective-permute-done((bf16[16,4096]{1,0:T(8,128)(2,1)S(1)}, bf16[16,4096]{1,0:T(8,128)(2,1)S(1)}, u32[]{:S(2)}, u32[]{:S(2)}) %collective-permute-start.5) | collective-permute-done | bytes 131104 | tf_op jit(solution)/shard_map/ppermute | solution.py:18
  35.0 4.6 %collective-permute-start.7 = (bf16[16,4096]{1,0:T(8,128)(2,1)S(1)}, bf16[16,4096]{1,0:T(8,128)(2,1)S(1)}, u32[]{:S(2)}, u32[]{:S(2)}) collective-permute-start(bf16[16,4096]{1,0:T(8,128)(2,1)S(1)} %collective-permute-done.5), channel_id=1, source_target_pairs={{0,15},{1,0},{2,1},{3,2},{4,3},{5,4},{6,5},{7,6},{8,7},{9,8},{10,9... | collective-permute-start | bytes 393224 | tf_op jit(solution)/shard_map/ppermute | solution.py:18
  39.9 2.2 %collective-permute-done.7 = bf16[16,4096]{1,0:T(8,128)(2,1)S(1)} collective-permute-done((bf16[16,4096]{1,0:T(8,128)(2,1)S(1)}, bf16[16,4096]{1,0:T(8,128)(2,1)S(1)}, u32[]{:S(2)}, u32[]{:S(2)}) %collective-permute-start.7) | collective-permute-done | bytes 131104 | tf_op jit(solution)/shard_map/ppermute | solution.py:18
  42.1 4.6 %collective-permute-start.9 = (bf16[16,4096]{1,0:T(8,128)(2,1)S(1)}, bf16[16,4096]{1,0:T(8,128)(2,1)}, u32[]{:S(2)}, u32[]{:S(2)}) collective-permute-start(bf16[16,4096]{1,0:T(8,128)(2,1)S(1)} %collective-permute-done.7), channel_id=1, source_target_pairs={{0,15},{1,0},{2,1},{3,2},{4,3},{5,4},{6,5},{7,6},{8,7},{9,8},{10,9... | collective-permute-start | bytes 393224 | tf_op jit(solution)/shard_map/ppermute | solution.py:18
  47.1 29.5 %all-gather.4.cloned.1.call-done = bf16[4096,768]{1,0:T(8,128)(2,1)} async-done(((bf16[256,768]{1,0:T(8,128)(2,1)}), bf16[4096,768]{1,0:T(8,128)(2,1)}) %all-gather.4.cloned.1.call-update) | async-done | bytes 6291472 | tf_op jit(solution)/shard_map/all_gather | solution.py:45
  76.6 9.1 %convolution_convert_fusion.1 = bf16[768,768]{0,1:T(8,128)(2,1)S(1)} fusion(bf16[768,4096]{1,0:T(8,128)(2,1)} %param.7, bf16[4096,768]{1,0:T(8,128)(2,1)} %all-gather.4.cloned.1.call-done), kind=kOutput, calls=%fused_computation.8 | convolution fusion | flops 4832428032 | bytes 13762560 | tf_op jit(solution)/shard_map/dot_general | solution.py:43
  87.7 1.9 %collective-permute-start.11 = (bf16[16,4096]{1,0:T(8,128)(2,1)}, bf16[16,4096]{1,0:T(8,128)(2,1)S(1)}, u32[]{:S(2)}, u32[]{:S(2)}) collective-permute-start(bf16[16,4096]{1,0:T(8,128)(2,1)} %collective-permute-done.9), channel_id=1, source_target_pairs={{0,15},{1,0},{2,1},{3,2},{4,3},{5,4},{6,5},{7,6},{8,7},{9,8},{10,9... | collective-permute-start | bytes 393224 | tf_op jit(solution)/shard_map/ppermute | solution.py:18
  91.4 1.0 collective-permute-done.11
  92.4 4.5 %collective-permute-start.13 = (bf16[16,4096]{1,0:T(8,128)(2,1)S(1)}, bf16[16,4096]{1,0:T(8,128)(2,1)S(1)}, u32[]{:S(2)}, u32[]{:S(2)}) collective-permute-start(bf16[16,4096]{1,0:T(8,128)(2,1)S(1)} %collective-permute-done.11), channel_id=1, source_target_pairs={{0,15},{1,0},{2,1},{3,2},{4,3},{5,4},{6,5},{7,6},{8,7},{9,8},{10,9... | collective-permute-start | bytes 393224 | tf_op jit(solution)/shard_map/ppermute | solution.py:18
  97.0 8.2 %collective-permute-done.12 = bf16[16,4096]{1,0:T(8,128)(2,1)S(1)} collective-permute-done((bf16[16,4096]{1,0:T(8,128)(2,1)S(1)}, bf16[16,4096]{1,0:T(8,128)(2,1)S(1)}, u32[]{:S(2)}, u32[]{:S(2)}) %collective-permute-start.12) | collective-permute-done | bytes 131104 | tf_op jit(solution)/shard_map/ppermute | solution.py:15
  105.3 7.0 %collective-permute-done.14 = bf16[16,4096]{1,0:T(8,128)(2,1)S(1)} collective-permute-done((bf16[16,4096]{1,0:T(8,128)(2,1)S(1)}, bf16[16,4096]{1,0:T(8,128)(2,1)S(1)}, u32[]{:S(2)}, u32[]{:S(2)}) %collective-permute-start.14) | collective-permute-done | bytes 131104 | tf_op jit(solution)/shard_map/ppermute | solution.py:15
  112.4 16.4 %all-gather.6.cloned.1.call-done = f32[32,128,128]{2,1,0:T(8,128)} async-done(((f32[2,128,128]{2,1,0:T(8,128)}), f32[32,128,128]{2,1,0:T(8,128)}) %all-gather.6.cloned.1.call-update) | async-done | bytes 2097168 | tf_op jit(solution)/shard_map/all_gather | solution.py:27
  128.8 14.6 %while.14 = (s32[]{:T(128)}, f32[2,128,128]{2,1,0:T(8,128)S(1)}, s32[]{:T(128)}, f32[16,2,128,128]{3,2,1,0:T(8,128)}, s32[]{:T(128)}, /*index=5*/s32[]{:T(128)}) while((s32[]{:T(128)}, f32[2,128,128]{2,1,0:T(8,128)S(1)}, s32[]{:T(128)}, f32[16,2,128,128]{3,2,1,0:T(8,128)}, s32[]{:T(128)}, /*index=5*/s32[]{:T(128)}) %tuple.42), condition=%wide.region_1.2_spmd.clone, body=%wide.region_0.1_spmd.clone.sunk | while | flops 98308 | bytes 393317 | solution.py:34
  129.7 0.9 add_select_fusion.2
  130.7 0.9 add_select_fusion.2
  131.7 0.9 add_select_fusion.2
  132.6 0.9 add_select_fusion.2
  133.6 0.9 add_select_fusion.2
  134.6 0.9 add_select_fusion.2
  135.6 0.9 add_select_fusion.2
  136.5 0.9 add_select_fusion.2
  137.5 0.9 add_select_fusion.2
  143.3 2.3 %fusion.7 = f32[2,128,768]{2,1,0:T(8,128)} fusion(bf16[768,2,128]{0,2,1:T(8,128)(2,1)S(1)} %bitcast.27, f32[2,128,128]{2,1,0:T(8,128)} %param.11, f32[2,128,128]{2,1,0:T(8,128)S(1)} %get-tuple-element.84), kind=kOutput, calls=%fused_computation.13 | convolution fusion | flops 302022656 | bytes 1441792 | tf_op jit(solution)/shard_map/thd,hde->the/dot_general | solution.py:64
  145.6 3.8 %multiply_reduce_fusion = (f32[768,2]{0,1:T(2,128)S(1)}, f32[768,2,128]{0,2,1:T(8,128)}) fusion(f32[2,128,768]{2,1,0:T(8,128)} %fusion.7, bf16[768,2,128]{0,2,1:T(8,128)(2,1)S(1)} %bitcast.24, bf16[768,2,128]{0,2,1:T(8,128)(2,1)S(1)} %bitcast.28, bf16[768,2,128]{0,2,1:T(8,128)(2,1)S(1)} %bitcast.26, pred[768,768]{1,0:T(8,128)(4,1)} %iota_compare_fusion), kind=kOutput, calls=%fused_computation.12 | convolution fusion | flops 606927360 | bytes 3348480 | tf_op jit(solution)/shard_map/hts,she->the/dot_general | solution.py:63
  149.5 1.2 multiply_convert_fusion
  150.7 4.5 %convolution_convert_fusion = bf16[768,4096]{1,0:T(8,128)(2,1)} fusion(bf16[768,256]{0,1:T(8,128)(2,1)S(1)} %bitcast.22, bf16[256,4096]{1,0:T(8,128)(2,1)S(1)} %constant_dynamic-update-slice_fusion), kind=kOutput, calls=%fused_computation.1 | convolution fusion | flops 1613758464 | bytes 8781824 | tf_op jit(solution)/shard_map/dot_general | solution.py:72
  (51 shorter events, 11.5 us)
Async XLA Ops:
  6.5 6.5 %copy-start = (bf16[16,4096]{1,0:T(8,128)(2,1)S(1)}, bf16[16,4096]{1,0:T(8,128)(2,1)}, u32[]{:S(2)}) copy-start(bf16[16,4096]{1,0:T(8,128)(2,1)} %param.9) | copy-start | bytes 393220
  6.5 70.1 %all-gather.4.cloned.1.call-start = ((), (), s32[]{:S(2)}) async-start(), calls=%async_computation | async-start | bytes 6684672 | tf_op jit(solution)/shard_map/all_gather | solution.py:45
  7.3 121.5 %all-gather.6.cloned.1.call-start = ((), (), s32[]{:S(2)}) async-start(), calls=%async_computation.1 | async-start | bytes 2228224 | tf_op jit(solution)/shard_map/all_gather | solution.py:27
  7.3 8.3 %collective-permute-start.1 = (bf16[16,4096]{1,0:T(8,128)(2,1)}, bf16[16,4096]{1,0:T(8,128)(2,1)S(1)}, u32[]{:S(2)}, u32[]{:S(2)}) collective-permute-start(bf16[16,4096]{1,0:T(8,128)(2,1)} %param.9), channel_id=1, source_target_pairs={{0,15},{1,0},{2,1},{3,2},{4,3},{5,4},{6,5},{7,6},{8,7},{9,8},{10,9... | collective-permute-start | bytes 393224 | tf_op jit(solution)/shard_map/ppermute | solution.py:18
  12.8 7.3 %collective-permute-start = (bf16[16,4096]{1,0:T(8,128)(2,1)}, bf16[16,4096]{1,0:T(8,128)(2,1)S(1)}, u32[]{:S(2)}, u32[]{:S(2)}) collective-permute-start(bf16[16,4096]{1,0:T(8,128)(2,1)} %param.9), channel_id=1, source_target_pairs={{0,1},{1,2},{2,3},{3,4},{4,5},{5,6},{6,7},{7,8},{8,9},{9,10},{10,1... | collective-permute-start | bytes 393224 | tf_op jit(solution)/shard_map/ppermute | solution.py:15
  15.6 9.7 %collective-permute-start.3 = (bf16[16,4096]{1,0:T(8,128)(2,1)S(1)}, bf16[16,4096]{1,0:T(8,128)(2,1)S(1)}, u32[]{:S(2)}, u32[]{:S(2)}) collective-permute-start(bf16[16,4096]{1,0:T(8,128)(2,1)S(1)} %collective-permute-done.1), channel_id=1, source_target_pairs={{0,15},{1,0},{2,1},{3,2},{4,3},{5,4},{6,5},{7,6},{8,7},{9,8},{10,9... | collective-permute-start | bytes 393224 | tf_op jit(solution)/shard_map/ppermute | solution.py:18
  20.1 9.9 %collective-permute-start.2 = (bf16[16,4096]{1,0:T(8,128)(2,1)S(1)}, bf16[16,4096]{1,0:T(8,128)(2,1)S(1)}, u32[]{:S(2)}, u32[]{:S(2)}) collective-permute-start(bf16[16,4096]{1,0:T(8,128)(2,1)S(1)} %collective-permute-done), channel_id=1, source_target_pairs={{0,1},{1,2},{2,3},{3,4},{4,5},{5,6},{6,7},{7,8},{8,9},{9,10},{10,1... | collective-permute-start | bytes 393224 | tf_op jit(solution)/shard_map/ppermute | solution.py:15
  25.3 9.7 %collective-permute-start.5 = (bf16[16,4096]{1,0:T(8,128)(2,1)S(1)}, bf16[16,4096]{1,0:T(8,128)(2,1)S(1)}, u32[]{:S(2)}, u32[]{:S(2)}) collective-permute-start(bf16[16,4096]{1,0:T(8,128)(2,1)S(1)} %collective-permute-done.3), channel_id=1, source_target_pairs={{0,15},{1,0},{2,1},{3,2},{4,3},{5,4},{6,5},{7,6},{8,7},{9,8},{10,9... | collective-permute-start | bytes 393224 | tf_op jit(solution)/shard_map/ppermute | solution.py:18
  30.0 9.9 %collective-permute-start.4 = (bf16[16,4096]{1,0:T(8,128)(2,1)S(1)}, bf16[16,4096]{1,0:T(8,128)(2,1)S(1)}, u32[]{:S(2)}, u32[]{:S(2)}) collective-permute-start(bf16[16,4096]{1,0:T(8,128)(2,1)S(1)} %collective-permute-done.2), channel_id=1, source_target_pairs={{0,1},{1,2},{2,3},{3,4},{4,5},{5,6},{6,7},{7,8},{8,9},{9,10},{10,1... | collective-permute-start | bytes 393224 | tf_op jit(solution)/shard_map/ppermute | solution.py:15
  35.0 7.1 %collective-permute-start.7 = (bf16[16,4096]{1,0:T(8,128)(2,1)S(1)}, bf16[16,4096]{1,0:T(8,128)(2,1)S(1)}, u32[]{:S(2)}, u32[]{:S(2)}) collective-permute-start(bf16[16,4096]{1,0:T(8,128)(2,1)S(1)} %collective-permute-done.5), channel_id=1, source_target_pairs={{0,15},{1,0},{2,1},{3,2},{4,3},{5,4},{6,5},{7,6},{8,7},{9,8},{10,9... | collective-permute-start | bytes 393224 | tf_op jit(solution)/shard_map/ppermute | solution.py:18
  39.9 7.3 %collective-permute-start.6 = (bf16[16,4096]{1,0:T(8,128)(2,1)S(1)}, bf16[16,4096]{1,0:T(8,128)(2,1)}, u32[]{:S(2)}, u32[]{:S(2)}) collective-permute-start(bf16[16,4096]{1,0:T(8,128)(2,1)S(1)} %collective-permute-done.4), channel_id=1, source_target_pairs={{0,1},{1,2},{2,3},{3,4},{4,5},{5,6},{6,7},{7,8},{8,9},{9,10},{10,1... | collective-permute-start | bytes 393224 | tf_op jit(solution)/shard_map/ppermute | solution.py:15
  42.1 45.5 %collective-permute-start.9 = (bf16[16,4096]{1,0:T(8,128)(2,1)S(1)}, bf16[16,4096]{1,0:T(8,128)(2,1)}, u32[]{:S(2)}, u32[]{:S(2)}) collective-permute-start(bf16[16,4096]{1,0:T(8,128)(2,1)S(1)} %collective-permute-done.7), channel_id=1, source_target_pairs={{0,15},{1,0},{2,1},{3,2},{4,3},{5,4},{6,5},{7,6},{8,7},{9,8},{10,9... | collective-permute-start | bytes 393224 | tf_op jit(solution)/shard_map/ppermute | solution.py:18
  47.1 42.5 %collective-permute-start.8 = (bf16[16,4096]{1,0:T(8,128)(2,1)}, bf16[16,4096]{1,0:T(8,128)(2,1)}, u32[]{:S(2)}, u32[]{:S(2)}) collective-permute-start(bf16[16,4096]{1,0:T(8,128)(2,1)} %collective-permute-done.6), channel_id=1, source_target_pairs={{0,1},{1,2},{2,3},{3,4},{4,5},{5,6},{6,7},{7,8},{8,9},{9,10},{10,1... | collective-permute-start | bytes 393224 | tf_op jit(solution)/shard_map/ppermute | solution.py:15
  87.7 4.7 %collective-permute-start.11 = (bf16[16,4096]{1,0:T(8,128)(2,1)}, bf16[16,4096]{1,0:T(8,128)(2,1)S(1)}, u32[]{:S(2)}, u32[]{:S(2)}) collective-permute-start(bf16[16,4096]{1,0:T(8,128)(2,1)} %collective-permute-done.9), channel_id=1, source_target_pairs={{0,15},{1,0},{2,1},{3,2},{4,3},{5,4},{6,5},{7,6},{8,7},{9,8},{10,9... | collective-permute-start | bytes 393224 | tf_op jit(solution)/shard_map/ppermute | solution.py:18
  89.6 7.4 %collective-permute-start.10 = (bf16[16,4096]{1,0:T(8,128)(2,1)}, bf16[16,4096]{1,0:T(8,128)(2,1)S(1)}, u32[]{:S(2)}, u32[]{:S(2)}) collective-permute-start(bf16[16,4096]{1,0:T(8,128)(2,1)} %collective-permute-done.8), channel_id=1, source_target_pairs={{0,1},{1,2},{2,3},{3,4},{4,5},{5,6},{6,7},{7,8},{8,9},{9,10},{10,1... | collective-permute-start | bytes 393224 | tf_op jit(solution)/shard_map/ppermute | solution.py:15
  92.4 12.9 %collective-permute-start.13 = (bf16[16,4096]{1,0:T(8,128)(2,1)S(1)}, bf16[16,4096]{1,0:T(8,128)(2,1)S(1)}, u32[]{:S(2)}, u32[]{:S(2)}) collective-permute-start(bf16[16,4096]{1,0:T(8,128)(2,1)S(1)} %collective-permute-done.11), channel_id=1, source_target_pairs={{0,15},{1,0},{2,1},{3,2},{4,3},{5,4},{6,5},{7,6},{8,7},{9,8},{10,9... | collective-permute-start | bytes 393224 | tf_op jit(solution)/shard_map/ppermute | solution.py:18
  97.0 8.3 %collective-permute-start.12 = (bf16[16,4096]{1,0:T(8,128)(2,1)S(1)}, bf16[16,4096]{1,0:T(8,128)(2,1)S(1)}, u32[]{:S(2)}, u32[]{:S(2)}) collective-permute-start(bf16[16,4096]{1,0:T(8,128)(2,1)S(1)} %collective-permute-done.10), channel_id=1, source_target_pairs={{0,1},{1,2},{2,3},{3,4},{4,5},{5,6},{6,7},{7,8},{8,9},{9,10},{10,1... | collective-permute-start | bytes 393224 | tf_op jit(solution)/shard_map/ppermute | solution.py:15
  105.3 7.1 %collective-permute-start.14 = (bf16[16,4096]{1,0:T(8,128)(2,1)S(1)}, bf16[16,4096]{1,0:T(8,128)(2,1)S(1)}, u32[]{:S(2)}, u32[]{:S(2)}) collective-permute-start(bf16[16,4096]{1,0:T(8,128)(2,1)S(1)} %collective-permute-done.12), channel_id=1, source_target_pairs={{0,1},{1,2},{2,3},{3,4},{4,5},{5,6},{6,7},{7,8},{8,9},{9,10},{10,1... | collective-permute-start | bytes 393224 | tf_op jit(solution)/shard_map/ppermute | solution.py:15
  145.6 3.8 %copy-start.1 = (f32[256]{0:T(256)S(1)}, f32[256]{0:T(256)}, u32[]{:S(2)}) copy-start(f32[256]{0:T(256)} %param.10) | copy-start | bytes 3076
Sparse Core Ops, SparseCore 0:
  9.6 66.9 all-gather.3
  86.8 41.8 all-gather.5
